TPU v7x, 32 devices: a whole 2x2x4 slice. The times are simulated.
32 devices in a mesh: slab: 4 (over z), sub: 8 (over y, x, core).
Axes of the slice: x: 2, y: 2, z: 4, core: 2. Of those that a mesh axis runs over, the one named last changes fastest.
Arguments:
- velocity_field: float32 [3, 64, 256, 512], P(None, 'slab', 'sub'), may hold values from -6 to 6
- particle_state: float32 [1024, 6, 256], P(('slab', 'sub')), as said below
- stokes_time: float32 [1024, 256], P(('slab', 'sub')), may hold values from 0.2 to 2
- box_base: int32 [1024, 3], P(('slab', 'sub')), may hold values from -2 to 511, as said below
- live_bins: int32 [32], P(('slab', 'sub')), may hold values from 1 to 32, as said below
Outputs:
- state_out: float32 [1024, 6, 256], P(('slab', 'sub'))
Inputs may be any that keep to these rules, and one draw needn't show every extreme that they name: `box_base`: columns 0 and 1 lie from -2 to 14 and from -2 to 30, column 2 from 0 to 511; bin 0 has column 0 at -2 and column 2 at 511. `live_bins`: some device has all 32 slots occupied. `particle_state`: positions lie in the box's central cell, 0 to 1 in each coordinate.
All inputs are finite; a program needn't handle non-finite values.
Results may differ from a plain program's by a relative error of at most 0.0003.
Values sent between devices are 32-bit elements; how exact they have to be, the bound alone decides.
No kernel may reach another device: no remote copies, remote signals or barrier semaphores. Data moves between devices by JAX's collectives and lax.ppermute only.
A program may use at most 64 MiB of HBM per device.

v0:
```python
import functools

import jax
import jax.numpy as jnp
from jax import lax
from jax.experimental import pallas as pl
from jax.experimental.pallas import tpu as pltpu
from jax.sharding import PartitionSpec as P

SUBSTEPS = 4
STEP_SIZE = 0.2
LANES = 128
NODES = 16
GROUP = 8
TOP = 8
UNROLL = 4
VMEM_LIMIT = 48 * 1024 * 1024


def rows_and_lanes():
    return lax.broadcasted_iota(jnp.int32, (8, LANES), 0), lax.broadcasted_iota(jnp.int32, (8, LANES), 1)


def gather_pair(planes, index, valid, nodes, first_row, first_z, slot):
    row, lane = rows_and_lanes()
    tiles = planes.shape[-3]
    tile, offset = first_z // LANES, first_z % LANES
    beside = (tile + 1) % tiles
    upper = row < 4
    first, second = index

    def load(at):
        return jnp.where(
            upper,
            planes[(*first, at, pl.ds(first_row, 8), slice(None))],
            planes[(*second, at, pl.ds(first_row - 4, 8), slice(None))],
        )

    rows = jnp.where(lane >= offset, load(tile), load(beside))
    rows = pltpu.roll(rows, (NODES * slot - first_z) & (LANES - 1), 1)
    wanted = jnp.where(upper, jnp.where(valid[0], 4 * slot, -1), jnp.where(valid[1], 4 * slot, -1))
    return rows, nodes & (lane // 4 == wanted)


def flatten_pair(parts):
    row, _ = rows_and_lanes()
    total = None
    for c, part in enumerate(parts):
        part = pltpu.roll(part, 0, 1, stride=4, stride_axis=0)
        part = part + pltpu.roll(part, 7, 0)
        part = part + pltpu.roll(part, 6, 0)
        part = jnp.where(row % 4 == 0, part, 0.0)
        part = pltpu.roll(part, c, 0) if c else part
        total = part if total is None else total + part
    return total


def align_pair(tile):
    row, _ = rows_and_lanes()
    return jnp.where(row < 4, tile, pltpu.roll(tile, LANES - NODES, 1))


def load_kernel(field, base, padded, near, far, table, sems):
    length, cells = field.shape[2:]
    even = lax.axis_index("sub") % 2 == 0

    def edge_copies(near_row, far_row):
        return [
            pltpu.make_async_copy(field.at[:, :, pl.ds(row, 2), :], into, sems.at[n])
            for n, (row, into) in enumerate(((near_row, near), (far_row, far)))
        ]

    @pl.when(even)
    def _():
        for copy in edge_copies(length - 2, 0):
            copy.start()

    @pl.when(jnp.logical_not(even))
    def _():
        for copy in edge_copies(0, length - 2):
            copy.start()

    copies = edge_copies(0, 0)
    copy = pltpu.make_async_copy(base, table, sems.at[2])
    copy.start()
    copies.append(copy)
    for tile in range(cells // LANES):
        copy = pltpu.make_async_copy(
            field.at[:, :, :, pl.ds(tile * LANES, LANES)],
            padded.at[:, :, tile, pl.ds(TOP, length), :],
            sems.at[3 + tile],
        )
        copy.start()
        copies.append(copy)
    for copy in copies:
        copy.wait()


def fill_halo(padded, far, near, planes):
    comps, _, tiles, rows, _ = padded.shape
    even = lax.axis_index("sub") % 2 == 0
    below, above = TOP - 2, rows - TOP
    near_row, far_row = jnp.where(even, above, below), jnp.where(even, below, above)
    for c in range(comps):
        for x in planes:
            for tile in range(tiles):
                lanes = slice(tile * LANES, (tile + 1) * LANES)
                padded[c, x, tile, pl.ds(near_row, 2), :] = near[c, x, :, lanes]
                padded[c, x, tile, pl.ds(far_row, 2), :] = far[c, x, :, lanes]


def own_nodes(first_y, length):
    row, _ = rows_and_lanes()
    node = row % 4 + first_y
    return (node >= 0) & (node < length)


def box_planes(first_x, pair, depth):
    x = [first_x + 2 * pair, first_x + 2 * pair + 1]
    return [jnp.clip(at, 0, depth - 1) for at in x], [(at >= 0) & (at < depth) for at in x]


def own_boxes_kernel(table, live, padded, box_table):
    comps, depth, _, rows, _ = padded.shape
    length = rows - 2 * TOP
    box_table[...] = jnp.zeros_like(box_table)

    def one_group(group, _):
        parts = [[jnp.zeros((8, LANES), jnp.float32)] * comps for _ in range(2)]
        for slot in range(GROUP):
            b = group * GROUP + slot
            first_x, first_y, first_z = table[0, b], table[1, b], table[2, b]
            nodes = own_nodes(first_y, length)
            for pair in range(2):
                x, valid = box_planes(first_x, pair, depth)
                for c in range(comps):
                    found, mask = gather_pair(
                        padded, ((c, x[0]), (c, x[1])), valid, nodes, TOP + first_y, first_z, slot
                    )
                    parts[pair][c] = jnp.where(mask, found, parts[pair][c])
        for pair in range(2):
            box_table[group, 8 * pair : 8 * pair + 8, :] = align_pair(flatten_pair(parts[pair]))
        return 0

    lax.fori_loop(0, (live[0] + GROUP - 1) // GROUP, one_group, 0)


def halo_boxes_kernel(table, live, far, near, partial, padded_in, box_table, padded, hits):
    comps, depth, _, rows, _ = padded.shape
    length = rows - 2 * TOP
    bins = table.shape[1]
    found = jnp.int32(0)
    for b in range(bins):
        hits[found] = b
        crossing = (table[1, b] < 0) | (table[1, b] > length - 4)
        found = found + (crossing & (b < live[0])).astype(jnp.int32)
    box_table[...] = partial[...]
    fill_halo(padded, far, near, range(2, depth - 2))

    def some_bins(n, _):
        for k in range(UNROLL):
            at = n * UNROLL + k
            b = hits[jnp.minimum(at, found - 1)]
            first_x, first_y, first_z = table[0, b], table[1, b], table[2, b]
            nodes = jnp.logical_not(own_nodes(first_y, length))
            for pair in range(2):
                x, valid = box_planes(first_x, pair, depth)
                valid = [v & (at < found) for v in valid]
                parts = []
                for c in range(comps):
                    gathered, mask = gather_pair(
                        padded, ((c, x[0]), (c, x[1])), valid, nodes, TOP + first_y, first_z, b % GROUP
                    )
                    parts.append(jnp.where(mask, gathered, 0.0))
                box_table[b // GROUP, 8 * pair : 8 * pair + 8, :] += align_pair(flatten_pair(parts))
        return 0

    lax.fori_loop(0, (found + UNROLL - 1) // UNROLL, some_bins, 0)


def answers_kernel(upper_table, lower_table, padded_in, far, near, before, upper_out, lower_out, padded, acc, hits):
    comps, depth, _, rows, _ = padded.shape
    bins = lower_table.shape[1]
    groups = bins // GROUP
    fill_halo(padded, far, near, [0, 1, depth - 2, depth - 1])
    acc[...] = jnp.zeros_like(acc)
    found = jnp.int32(0)
    for side, table in enumerate((upper_table, lower_table)):
        for b in range(bins):
            hits[found] = side * bins + b
            wanted = table[0, b] > depth - 4 if side else table[0, b] < 0
            found = found + wanted.astype(jnp.int32)

    def some_bins(n, _):
        for k in range(UNROLL):
            at = n * UNROLL + k
            entry = hits[jnp.minimum(at, found - 1)]
            side, b = entry // bins, entry % bins
            first_x, first_y, first_z = [jnp.where(side == 0, upper_table[d, b], lower_table[d, b]) for d in range(3)]
            x = first_x + jnp.where(side == 0, depth, 2 - depth)
            x = [x, x + 1]
            valid = [(at < found) & (cell >= 0) & (cell < depth) for cell in x]
            x = [jnp.clip(cell, 0, depth - 1) for cell in x]
            parts = []
            for c in range(comps):
                gathered, mask = gather_pair(
                    padded, ((c, x[0]), (c, x[1])), valid, True, TOP + first_y, first_z, b % GROUP
                )
                parts.append(jnp.where(mask, gathered, 0.0))
            acc[side * groups + b // GROUP] += flatten_pair(parts)
        return 0

    lax.fori_loop(0, (found + UNROLL - 1) // UNROLL, some_bins, 0)
    for g in range(groups):
        upper_out[g] = align_pair(acc[g])
        lower_out[g] = align_pair(acc[groups + g])


def unscaled_weights(t):
    plus, minus, minus_two = t + 1.0, t - 1.0, t - 2.0
    inner, outer = t * minus, plus * minus_two
    return inner * minus_two, outer * minus, outer * t, inner * plus


def node_factor(node):
    return jnp.where(node == 0, -1.0 / 6.0, jnp.where(node == 1, 0.5, jnp.where(node == 2, -0.5, 1.0 / 6.0)))


def split(x):
    head = x.astype(jnp.bfloat16)
    return head, (x - head.astype(jnp.float32)).astype(jnp.bfloat16)


def group_matrix(box):
    row = lax.broadcasted_iota(jnp.int32, box.shape, 0)
    lane = lax.broadcasted_iota(jnp.int32, box.shape, 1)
    box = box * (node_factor(row // 4) * node_factor(lane // 4 % 4) * node_factor(lane % 4))
    box = jnp.take_along_axis(box, lane % GROUP * NODES + lane // GROUP, axis=1)
    head = box.astype(jnp.bfloat16).astype(jnp.float32)
    own = lax.broadcasted_iota(jnp.int32, (GROUP, LANES), 1) % GROUP == lax.broadcasted_iota(
        jnp.int32, (GROUP, LANES), 0
    )

    def spread(part):
        rows = [
            jnp.where(own, jnp.broadcast_to(part[4 * i + c : 4 * i + c + 1], (GROUP, LANES)), 0.0)
            for i in range(4)
            for c in range(3)
        ]
        return jnp.concatenate(rows, axis=0).astype(jnp.bfloat16)

    heads, tails = spread(head), spread(box - head)
    return jnp.concatenate([heads, heads, tails], axis=1)


def sample(matrix, position):
    along_x, along_y, along_z = (unscaled_weights(t) for t in position)
    weights = jnp.concatenate([y * z for y in along_y for z in along_z], axis=0)
    head, tail = split(weights)
    planes = jnp.dot(
        matrix, jnp.concatenate([head, tail, head], axis=0), preferred_element_type=jnp.float32
    )
    result = []
    for c in range(3):
        plane = [planes[8 * (3 * i + c) : 8 * (3 * i + c) + 8] for i in range(4)]
        result.append(
            (plane[0] * along_x[0] + plane[1] * along_x[1]) + (plane[2] * along_x[2] + plane[3] * along_x[3])
        )
    return result


def move_kernel(live, box_table, from_lower, from_upper, state, stokes, out):
    groups = box_table.shape[0]
    count = live[0]
    matrices, carry, rates, alive = [], [], [], []
    for g in range(groups):
        rows = slice(g * GROUP, (g + 1) * GROUP)
        answers = jnp.concatenate([from_lower[g], from_upper[g]], axis=0)
        matrices.append(group_matrix(box_table[g] + answers))
        rates.append(1.0 / stokes[rows, :])
        kept = g * GROUP + lax.broadcasted_iota(jnp.int32, rates[g].shape, 0) < count
        alive.append(kept)
        start = [jnp.where(kept, state[c, rows, :], 0.0) for c in range(6)]
        carry.append((start[:3], start[3:]))

    for _ in range(SUBSTEPS):
        moved = []
        for g in range(groups):
            position, velocity = carry[g]
            rate = rates[g]
            middle_pos = [x + 0.5 * STEP_SIZE * v for x, v in zip(position, velocity)]
            here = sample(matrices[g], position)
            there = sample(matrices[g], middle_pos)
            middle_vel = [v + 0.5 * STEP_SIZE * ((u - v) * rate) for u, v in zip(here, velocity)]
            moved.append(
                (
                    [x + STEP_SIZE * m for x, m in zip(position, middle_vel)],
                    [v + STEP_SIZE * (u - m) * rate for v, u, m in zip(velocity, there, middle_vel)],
                )
            )
        carry = moved
    for g in range(groups):
        rows = slice(g * GROUP, (g + 1) * GROUP)
        for c, value in enumerate([*carry[g][0], *carry[g][1]]):
            out[c, rows, :] = jnp.where(alive[g], value, state[c, rows, :])


def in_smem():
    return pl.BlockSpec(memory_space=pltpu.SMEM)


def in_vmem():
    return pl.BlockSpec(memory_space=pltpu.VMEM)


def exchange(near, far, axis):
    devices = lax.axis_size(axis)
    near_pairs = [(i, i ^ 1) for i in range(devices)]
    far_pairs = [(i, (i + 1 if i % 2 else i - 1) % devices) for i in range(devices)]
    far = lax.ppermute(far, axis, far_pairs)
    return lax.ppermute(near, axis, near_pairs), far


def shift(array, axis, step):
    devices = lax.axis_size(axis)
    return lax.ppermute(array, axis, [(i, (i + step) % devices) for i in range(devices)])


def body(velocity_field, particle_state, stokes_time, box_base, live_bins):
    comps, depth, length, cells = velocity_field.shape
    bins = box_base.shape[0]
    tiles = cells // LANES
    groups = bins // GROUP
    table = box_base.T
    state = particle_state.transpose(1, 0, 2)
    block = pltpu.with_memory_space_constraint(velocity_field, pltpu.HBM)
    params = pltpu.CompilerParams(vmem_limit_bytes=VMEM_LIMIT)

    lower_table, upper_table = shift(table, "slab", 1), shift(table, "slab", -1)
    padded_block = pltpu.VMEM((comps, depth, tiles, length + 2 * TOP, LANES), jnp.float32)
    edge_rows = jax.ShapeDtypeStruct((comps, depth, 2, cells), jnp.float32)
    padded, near, far, own_table = pl.pallas_call(
        load_kernel,
        out_shape=(
            padded_block,
            edge_rows,
            edge_rows,
            pltpu.SMEM(table.shape, jnp.int32),
        ),
        in_specs=[pl.BlockSpec(memory_space=pl.ANY)] * 2,
        out_specs=(in_vmem(), in_vmem(), in_vmem(), in_smem()),
        scratch_shapes=[pltpu.SemaphoreType.DMA((3 + tiles,))],
        compiler_params=params,
        name="load",
    )(block, pltpu.with_memory_space_constraint(table, pltpu.HBM))
    near, far = exchange(near, far, "sub")

    box_tables = jax.ShapeDtypeStruct((groups, NODES, LANES), jnp.float32)
    box_table = pl.pallas_call(
        own_boxes_kernel,
        out_shape=box_tables,
        in_specs=[in_smem(), in_smem(), in_vmem()],
        out_specs=in_vmem(),
        compiler_params=params,
        cost_estimate=pl.CostEstimate(flops=1_000_000, bytes_accessed=8_000_000, transcendentals=0),
        name="own_boxes",
    )(own_table, live_bins, padded)

    answer = jax.ShapeDtypeStruct((groups, 8, LANES), jnp.float32)
    for_upper, for_lower, padded = pl.pallas_call(
        answers_kernel,
        out_shape=(answer, answer, padded_block),
        in_specs=[in_smem(), in_smem(), in_vmem(), in_vmem(), in_vmem(), pl.BlockSpec(memory_space=pl.ANY)],
        out_specs=(in_vmem(), in_vmem(), in_vmem()),
        scratch_shapes=[pltpu.VMEM((2 * groups, 8, LANES), jnp.float32), pltpu.SMEM((2 * bins + 1,), jnp.int32)],
        input_output_aliases={2: 2},
        compiler_params=params,
        name="answers",
    )(upper_table, lower_table, padded, far, near, box_table)
    from_lower, from_upper = shift(for_upper, "slab", 1), shift(for_lower, "slab", -1)

    box_table, _ = pl.pallas_call(
        halo_boxes_kernel,
        out_shape=(box_tables, padded_block),
        in_specs=[in_smem(), in_smem(), in_vmem(), in_vmem(), in_vmem(), in_vmem()],
        out_specs=(in_vmem(), in_vmem()),
        scratch_shapes=[pltpu.SMEM((bins + 1,), jnp.int32)],
        input_output_aliases={5: 1},
        compiler_params=params,
        cost_estimate=pl.CostEstimate(flops=1_000_000, bytes_accessed=4_000_000, transcendentals=0),
        name="halo_boxes",
    )(own_table, live_bins, far, near, box_table, padded)

    moved = pl.pallas_call(
        move_kernel,
        out_shape=jax.ShapeDtypeStruct(state.shape, jnp.float32),
        in_specs=[in_smem()] + [in_vmem()] * 5,
        out_specs=in_vmem(),
        compiler_params=params,
        name="move",
    )(live_bins, box_table, from_lower, from_upper, state, stokes_time)
    return moved.transpose(1, 0, 2)


def solution(mesh):
    placed = (
        P(None, "slab", "sub", None),
        P(("slab", "sub"), None, None),
        P(("slab", "sub"), None),
        P(("slab", "sub"), None),
        P(("slab", "sub")),
    )
    return jax.shard_map(
        body, mesh=mesh, in_specs=placed, out_specs=P(("slab", "sub"), None, None), check_vma=False
    )
```

profile of v0, /device:TPU:0, one launch (start us, length us, event | category | flops | bytes accessed | tf_op | source)
XLA Modules:
  0.0 21.3 jit_solution(9412754170714694455)
XLA Ops:
  0.0 2.2 %load.1 = (f32[3,16,4,48,128]{4,3,2,1,0:T(8,128)S(1)}, f32[3,16,2,512]{3,2,1,0:T(2,128)S(1)}, f32[3,16,2,512]{3,2,1,0:T(2,128)S(1)}, s32[3,32]{1,0:T(4,128)S(4)}) custom-call(f32[3,16,32,512]{3,2,1,0:T(8,128)} %field.1, s32[3,32]{1,0:T(4,128)} %bitcast.4), custom_call_target="tpu_custom_call" | custom-call | tf_op jit(solution)/shard_map/load/pallas_call | solution.py:342
  2.2 3.4 %collective-permute-start = (f32[3,16,2,512]{3,2,1,0:T(2,128)S(1)}, f32[3,16,2,512]{3,2,1,0:T(2,128)S(1)}, u32[]{:S(2)}, u32[]{:S(2)}) collective-permute-start(f32[3,16,2,512]{3,2,1,0:T(2,128)S(1)} %get-tuple-element.14), channel_id=1, source_target_pairs={{0,7},{1,2},{2,1},{3,4},{4,3},{5,6},{6,5},{7,0},{8,15},{9,10},{10,... | collective-permute-start | bytes 589832 | tf_op jit(solution)/shard_map/ppermute | solution.py:320
  5.6 0.0 collective-permute-start.1
  5.6 1.6 %collective-permute-start.3 = (s32[3,32]{1,0:T(4,128)}, s32[3,32]{1,0:T(4,128)S(1)}, u32[]{:S(2)}, u32[]{:S(2)}) collective-permute-start(s32[3,32]{1,0:T(4,128)} %bitcast.5), channel_id=1, source_target_pairs={{0,8},{8,16},{16,24},{24,0},{1,9},{9,17},{17,25},{25,1},{2,10},{10... | collective-permute-start | bytes 1160 | tf_op jit(solution)/shard_map/ppermute | solution.py:326
  7.2 2.2 %collective-permute-start.2 = (s32[3,32]{1,0:T(4,128)}, s32[3,32]{1,0:T(4,128)S(1)}, u32[]{:S(2)}, u32[]{:S(2)}) collective-permute-start(s32[3,32]{1,0:T(4,128)} %bitcast.6), channel_id=1, source_target_pairs={{0,24},{8,0},{16,8},{24,16},{1,25},{9,1},{17,9},{25,17},{2,26},{10... | collective-permute-start | bytes 1160 | tf_op jit(solution)/shard_map/ppermute | solution.py:326
  10.1 0.4 %own_boxes.1.before.partial = f32[4,16,128]{2,1,0:T(8,128)S(1)} custom-call(s32[3,32]{1,0:T(4,128)S(4)} %get-tuple-element.13.table, s32[1]{0:T(128)S(6)} %copy.10.live, f32[3,16,4,48,128]{4,3,2,1,0:T(8,128)S(1)} %get-tuple-element.16.padded.padded_in), custom_call_target="tpu_custom_call" | custom-call | flops 1000000 | bytes 8000000 | tf_op jit(solution)/shard_map/own_boxes/pallas_call | solution.py:359
  10.5 0.0 copy-start
  10.5 0.0 copy-start.1
  10.5 0.7 %collective-permute-done.3.lower_table = s32[3,32]{1,0:T(4,128)S(1)} collective-permute-done((s32[3,32]{1,0:T(4,128)}, s32[3,32]{1,0:T(4,128)S(1)}, u32[]{:S(2)}, u32[]{:S(2)}) %collective-permute-start.3) | collective-permute-done | bytes 416 | tf_op jit(solution)/shard_map/ppermute | solution.py:326
  11.2 0.0 collective-permute-done.2.upper_table
  11.2 0.0 collective-permute-done.far
  11.2 0.0 collective-permute-done.1.near
  11.2 1.6 %answers.1 = (f32[4,8,128]{2,1,0:T(8,128)S(1)}, f32[4,8,128]{2,1,0:T(8,128)S(1)}, f32[3,16,4,48,128]{4,3,2,1,0:T(8,128)S(1)}) custom-call(s32[3,32]{1,0:T(4,128)S(1)} %collective-permute-done.2.upper_table, s32[3,32]{1,0:T(4,128)S(1)} %collective-permute-done.3.lower_table, ...), custom_call_target="tpu_custom_call", output_to_operand_aliasing={{2}: (2, {})} | custom-call | tf_op jit(solution)/shard_map/answers/pallas_call | solution.py:370
  12.8 1.8 %collective-permute-start.4 = (f32[4,8,128]{2,1,0:T(8,128)S(1)}, f32[4,8,128]{2,1,0:T(8,128)S(1)}, u32[]{:S(2)}, u32[]{:S(2)}) collective-permute-start(f32[4,8,128]{2,1,0:T(8,128)S(1)} %get-tuple-element.19), channel_id=1, source_target_pairs={{0,8},{8,16},{16,24},{24,0},{1,9},{9,17},{17,25},{25,1},{2,10},{10... | collective-permute-start | bytes 49160 | tf_op jit(solution)/shard_map/ppermute | solution.py:326
  14.7 2.6 %collective-permute-start.5 = (f32[4,8,128]{2,1,0:T(8,128)S(1)}, f32[4,8,128]{2,1,0:T(8,128)S(1)}, u32[]{:S(2)}, u32[]{:S(2)}) collective-permute-start(f32[4,8,128]{2,1,0:T(8,128)S(1)} %get-tuple-element.20), channel_id=1, source_target_pairs={{0,24},{8,0},{16,8},{24,16},{1,25},{9,1},{17,9},{25,17},{2,26},{10... | collective-permute-start | bytes 49160 | tf_op jit(solution)/shard_map/ppermute | solution.py:326
  17.3 0.5 %halo_boxes.1 = (f32[4,16,128]{2,1,0:T(8,128)S(1)}, f32[3,16,4,48,128]{4,3,2,1,0:T(8,128)S(1)}) custom-call(s32[3,32]{1,0:T(4,128)S(4)} %get-tuple-element.13.table, s32[1]{0:T(128)S(6)} %copy.10.live, f32[3,16,2,512]{3,2,1,0:T(2,128)S(1)} %collective-permute-done.far, ...), custom_call_target="tpu_custom_call", output_to_operand_aliasing={{1}: (5, {})} | custom-call | flops 1000000 | bytes 4000000 | tf_op jit(solution)/shard_map/halo_boxes/pallas_call | solution.py:382
  17.8 1.1 %collective-permute-done.4.from_lower = f32[4,8,128]{2,1,0:T(8,128)S(1)} collective-permute-done((f32[4,8,128]{2,1,0:T(8,128)S(1)}, f32[4,8,128]{2,1,0:T(8,128)S(1)}, u32[]{:S(2)}, u32[]{:S(2)}) %collective-permute-start.4) | collective-permute-done | bytes 16416 | tf_op jit(solution)/shard_map/ppermute | solution.py:326
  18.9 0.0 collective-permute-done.5.from_upper
  18.9 0.0 copy-done
  18.9 0.0 copy-done.1
  18.9 2.4 %move.1 = f32[6,32,256]{2,1,0:T(8,128)} custom-call(s32[1]{0:T(128)S(6)} %copy.10.live, f32[4,16,128]{2,1,0:T(8,128)S(1)} %get-tuple-element.18.box_table, f32[4,8,128]{2,1,0:T(8,128)S(1)} %collective-permute-done.4.from_lower, f32[4,8,128]{2,1,0:T(8,128)S(1)} %collective-permute-done.5.from_upper, f32[6,32,256]{2,1,0:T(8,128)S(1)} %bitcast.3, ...), custom_call_target="tpu_custom_call" | custom-call | tf_op jit(solution)/shard_map/move/pallas_call | solution.py:394
Async XLA Ops:
  2.2 9.0 %collective-permute-start = (f32[3,16,2,512]{3,2,1,0:T(2,128)S(1)}, f32[3,16,2,512]{3,2,1,0:T(2,128)S(1)}, u32[]{:S(2)}, u32[]{:S(2)}) collective-permute-start(f32[3,16,2,512]{3,2,1,0:T(2,128)S(1)} %get-tuple-element.14), channel_id=1, source_target_pairs={{0,7},{1,2},{2,1},{3,4},{4,3},{5,6},{6,5},{7,0},{8,15},{9,10},{10,... | collective-permute-start | bytes 589832 | tf_op jit(solution)/shard_map/ppermute | solution.py:320
  5.6 5.6 %collective-permute-start.1 = (f32[3,16,2,512]{3,2,1,0:T(2,128)S(1)}, f32[3,16,2,512]{3,2,1,0:T(2,128)S(1)}, u32[]{:S(2)}, u32[]{:S(2)}) collective-permute-start(f32[3,16,2,512]{3,2,1,0:T(2,128)S(1)} %get-tuple-element.15), channel_id=1, source_target_pairs={{0,1},{1,0},{2,3},{3,2},{4,5},{5,4},{6,7},{7,6},{8,9},{9,8},{10,11... | collective-permute-start | bytes 589832 | tf_op jit(solution)/shard_map/ppermute | solution.py:321
  5.6 5.6 %collective-permute-start.3 = (s32[3,32]{1,0:T(4,128)}, s32[3,32]{1,0:T(4,128)S(1)}, u32[]{:S(2)}, u32[]{:S(2)}) collective-permute-start(s32[3,32]{1,0:T(4,128)} %bitcast.5), channel_id=1, source_target_pairs={{0,8},{8,16},{16,24},{24,0},{1,9},{9,17},{17,25},{25,1},{2,10},{10... | collective-permute-start | bytes 1160 | tf_op jit(solution)/shard_map/ppermute | solution.py:326
  7.2 4.0 %collective-permute-start.2 = (s32[3,32]{1,0:T(4,128)}, s32[3,32]{1,0:T(4,128)S(1)}, u32[]{:S(2)}, u32[]{:S(2)}) collective-permute-start(s32[3,32]{1,0:T(4,128)} %bitcast.6), channel_id=1, source_target_pairs={{0,24},{8,0},{16,8},{24,16},{1,25},{9,1},{17,9},{25,17},{2,26},{10... | collective-permute-start | bytes 1160 | tf_op jit(solution)/shard_map/ppermute | solution.py:326
  10.5 8.4 %copy-start = (f32[32,6,256]{2,0,1:T(8,128)S(1)}, f32[32,6,256]{2,0,1:T(8,128)}, u32[]{:S(2)}) copy-start(f32[32,6,256]{2,0,1:T(8,128)} %param.6) | copy-start | bytes 589828
  10.5 8.4 %copy-start.1 = (f32[32,256]{1,0:T(8,128)S(1)}, f32[32,256]{1,0:T(8,128)}, u32[]{:S(2)}) copy-start(f32[32,256]{1,0:T(8,128)} %stokes.1) | copy-start | bytes 98308
  12.8 6.1 %collective-permute-start.4 = (f32[4,8,128]{2,1,0:T(8,128)S(1)}, f32[4,8,128]{2,1,0:T(8,128)S(1)}, u32[]{:S(2)}, u32[]{:S(2)}) collective-permute-start(f32[4,8,128]{2,1,0:T(8,128)S(1)} %get-tuple-element.19), channel_id=1, source_target_pairs={{0,8},{8,16},{16,24},{24,0},{1,9},{9,17},{17,25},{25,1},{2,10},{10... | collective-permute-start | bytes 49160 | tf_op jit(solution)/shard_map/ppermute | solution.py:326
  14.7 4.3 %collective-permute-start.5 = (f32[4,8,128]{2,1,0:T(8,128)S(1)}, f32[4,8,128]{2,1,0:T(8,128)S(1)}, u32[]{:S(2)}, u32[]{:S(2)}) collective-permute-start(f32[4,8,128]{2,1,0:T(8,128)S(1)} %get-tuple-element.20), channel_id=1, source_target_pairs={{0,24},{8,0},{16,8},{24,16},{1,25},{9,1},{17,9},{25,17},{2,26},{10... | collective-permute-start | bytes 49160 | tf_op jit(solution)/shard_map/ppermute | solution.py:326
where the time goes:
time: 21.6 us; the launch traced here: 21.3 us
  starting transfers between devices  11.6 us (54%)
  Pallas kernels  7.18 us (33%)
  waiting for transfers between devices  1.8 us (8%)
  between operations  0.68 us (3%)
    ppermute x4, starting transfers between devices, shift(): lax.ppermute(array, axis, [(i, (i + step) % devices) for i in range(devic...  8.24 us
    ppermute x1, starting transfers between devices, exchange(): far = lax.ppermute(far, axis, far_pairs)  3.4 us
    pallas_call x1, Pallas kernels, body(): pl.pallas_call(move_kernel, out_shape=jax.ShapeDtypeStruct(state.shape, j...  2.39 us
    pallas_call x1, Pallas kernels, body(): pl.pallas_call(load_kernel, out_shape=(padded_block, edge_rows, edge_rows...  2.18 us
    ppermute x4, waiting for transfers between devices, shift(): lax.ppermute(array, axis, [(i, (i + step) % devices) for i in range(devic...  1.79 us
    pallas_call x1, Pallas kernels, body(): pl.pallas_call(answers_kernel, out_shape=(answer, answer, padded_block),...  1.64 us
    pallas_call x1, Pallas kernels, body(): pl.pallas_call(halo_boxes_kernel, out_shape=(box_tables, padded_block), i...  0.54 us
    pallas_call x1, Pallas kernels, body(): pl.pallas_call(own_boxes_kernel, out_shape=box_tables, in_specs=[in_smem(...  0.44 us
  transfers between devices with their start and end apart: 6, of which 2 were waited for; matrix products, arithmetic and copies ran while one was open for 0% of the time, Pallas kernels for 5%

commit v1 on v0

--- a/solution.py
+++ b/solution.py
@@ -10,8 +10,10 @@
 SUBSTEPS = 4
 STEP_SIZE = 0.2
 LANES = 128
+LANE_BITS = 7
 NODES = 16
 GROUP = 8
+GROUP_BITS = 3
 TOP = 8
 UNROLL = 4
 VMEM_LIMIT = 48 * 1024 * 1024
@@ -24,8 +26,8 @@
 def gather_pair(planes, index, valid, nodes, first_row, first_z, slot):
     row, lane = rows_and_lanes()
     tiles = planes.shape[-3]
-    tile, offset = first_z // LANES, first_z % LANES
-    beside = (tile + 1) % tiles
+    tile, offset = lax.shift_right_logical(first_z, LANE_BITS), first_z & (LANES - 1)
+    beside = jnp.where(tile == tiles - 1, 0, tile + 1)
     upper = row < 4
     first, second = index
 
@@ -39,7 +41,7 @@
     rows = jnp.where(lane >= offset, load(tile), load(beside))
     rows = pltpu.roll(rows, (NODES * slot - first_z) & (LANES - 1), 1)
     wanted = jnp.where(upper, jnp.where(valid[0], 4 * slot, -1), jnp.where(valid[1], 4 * slot, -1))
-    return rows, nodes & (lane // 4 == wanted)
+    return rows, nodes & (lax.shift_right_logical(lane, 2) == wanted)
 
 
 def flatten_pair(parts):
@@ -49,7 +51,7 @@
         part = pltpu.roll(part, 0, 1, stride=4, stride_axis=0)
         part = part + pltpu.roll(part, 7, 0)
         part = part + pltpu.roll(part, 6, 0)
-        part = jnp.where(row % 4 == 0, part, 0.0)
+        part = jnp.where((row & 3) == 0, part, 0.0)
         part = pltpu.roll(part, c, 0) if c else part
         total = part if total is None else total + part
     return total
@@ -111,7 +113,7 @@
 
 def own_nodes(first_y, length):
     row, _ = rows_and_lanes()
-    node = row % 4 + first_y
+    node = (row & 3) + first_y
     return (node >= 0) & (node < length)
 
 
@@ -169,10 +171,10 @@
                 parts = []
                 for c in range(comps):
                     gathered, mask = gather_pair(
-                        padded, ((c, x[0]), (c, x[1])), valid, nodes, TOP + first_y, first_z, b % GROUP
+                        padded, ((c, x[0]), (c, x[1])), valid, nodes, TOP + first_y, first_z, b & (GROUP - 1)
                     )
                     parts.append(jnp.where(mask, gathered, 0.0))
-                box_table[b // GROUP, 8 * pair : 8 * pair + 8, :] += align_pair(flatten_pair(parts))
+                box_table[lax.shift_right_logical(b, GROUP_BITS), 8 * pair : 8 * pair + 8, :] += align_pair(flatten_pair(parts))
         return 0
 
     lax.fori_loop(0, (found + UNROLL - 1) // UNROLL, some_bins, 0)
@@ -195,25 +197,28 @@
         for k in range(UNROLL):
             at = n * UNROLL + k
             entry = hits[jnp.minimum(at, found - 1)]
-            side, b = entry // bins, entry % bins
-            first_x, first_y, first_z = [jnp.where(side == 0, upper_table[d, b], lower_table[d, b]) for d in range(3)]
-            x = first_x + jnp.where(side == 0, depth, 2 - depth)
+            from_upper = entry < bins
+            b = jnp.where(from_upper, entry, entry - bins)
+            first_x, first_y, first_z = [jnp.where(from_upper, upper_table[d, b], lower_table[d, b]) for d in range(3)]
+            x = first_x + jnp.where(from_upper, depth, 2 - depth)
             x = [x, x + 1]
             valid = [(at < found) & (cell >= 0) & (cell < depth) for cell in x]
             x = [jnp.clip(cell, 0, depth - 1) for cell in x]
             parts = []
             for c in range(comps):
                 gathered, mask = gather_pair(
-                    padded, ((c, x[0]), (c, x[1])), valid, True, TOP + first_y, first_z, b % GROUP
+                    padded, ((c, x[0]), (c, x[1])), valid, True, TOP + first_y, first_z, b & (GROUP - 1)
                 )
                 parts.append(jnp.where(mask, gathered, 0.0))
-            acc[side * groups + b // GROUP] += flatten_pair(parts)
+            group = lax.shift_right_logical(entry, GROUP_BITS)
+            for c in range(comps):
+                acc[group, c] += parts[c]
         return 0
 
     lax.fori_loop(0, (found + UNROLL - 1) // UNROLL, some_bins, 0)
     for g in range(groups):
-        upper_out[g] = align_pair(acc[g])
-        lower_out[g] = align_pair(acc[groups + g])
+        upper_out[g] = align_pair(flatten_pair([acc[g, c] for c in range(comps)]))
+        lower_out[g] = align_pair(flatten_pair([acc[groups + g, c] for c in range(comps)]))
 
 
 def unscaled_weights(t):
@@ -269,9 +274,7 @@
     return result
 
 
-def move_kernel(live, box_table, from_lower, from_upper, state, stokes, out):
-    groups = box_table.shape[0]
-    count = live[0]
+def move_groups(groups, count, box_table, from_lower, from_upper, state, stokes, out):
     matrices, carry, rates, alive = [], [], [], []
     for g in range(groups):
         rows = slice(g * GROUP, (g + 1) * GROUP)
@@ -282,7 +285,6 @@
         alive.append(kept)
         start = [jnp.where(kept, state[c, rows, :], 0.0) for c in range(6)]
         carry.append((start[:3], start[3:]))
-
     for _ in range(SUBSTEPS):
         moved = []
         for g in range(groups):
@@ -303,6 +305,21 @@
         rows = slice(g * GROUP, (g + 1) * GROUP)
         for c, value in enumerate([*carry[g][0], *carry[g][1]]):
             out[c, rows, :] = jnp.where(alive[g], value, state[c, rows, :])
+    if groups < box_table.shape[0]:
+        out[:, groups * GROUP :, :] = state[:, groups * GROUP :, :]
+
+
+def move_kernel(live, box_table, from_lower, from_upper, state, stokes, out):
+    count = live[0]
+    groups = box_table.shape[0]
+    fewer = 0
+    for some in sorted({1, max(1, groups // 2), groups}):
+
+        @pl.when((count > fewer * GROUP) & (count <= some * GROUP))
+        def _(some=some):
+            move_groups(some, count, box_table, from_lower, from_upper, state, stokes, out)
+
+        fewer = some
 
 
 def in_smem():
@@ -372,7 +389,10 @@
         out_shape=(answer, answer, padded_block),
         in_specs=[in_smem(), in_smem(), in_vmem(), in_vmem(), in_vmem(), pl.BlockSpec(memory_space=pl.ANY)],
         out_specs=(in_vmem(), in_vmem(), in_vmem()),
-        scratch_shapes=[pltpu.VMEM((2 * groups, 8, LANES), jnp.float32), pltpu.SMEM((2 * bins + 1,), jnp.int32)],
+        scratch_shapes=[
+            pltpu.VMEM((2 * groups, comps, 8, LANES), jnp.float32),
+            pltpu.SMEM((2 * bins + 1,), jnp.int32),
+        ],
         input_output_aliases={2: 2},
         compiler_params=params,
         name="answers",

time: 21.6 us -> 20.4 us (0.944)
  Pallas kernels: 7.18 us -> 6.48 us
    pallas_call x1, Pallas kernels: 2.39 us -> 1.82 us  [body(): pl.pallas_call(move_kernel, out_shape=jax.ShapeDtypeStruct(state.shape, j...]
    pallas_call x1, Pallas kernels: 1.64 us -> 1.23 us  [body(): pl.pallas_call(answers_kernel, out_shape=(answer, answer, padded_block),...]
    pallas_call x1, Pallas kernels: 0.44 us -> 0.76 us  [body(): pl.pallas_call(own_boxes_kernel, out_shape=box_tables, in_specs=[in_smem(...]
  transfers between devices with their start and end apart: 6 -> 6, of which waited for: 2 -> 3; matrix products, arithmetic and copies ran while one was open for 0% -> 0% of each run, Pallas kernels for 5% -> 6%
where the time goes in v1:
time: 20.4 us; the launch traced here: 20.3 us
  starting transfers between devices  11.4 us (56%)
  Pallas kernels  6.48 us (32%)
  waiting for transfers between devices  1.69 us (8%)
  between operations  0.68 us (3%)
    ppermute x4, starting transfers between devices, shift(): lax.ppermute(array, axis, [(i, (i + step) % devices) for i in range(devic...  8.04 us
    ppermute x1, starting transfers between devices, exchange(): far = lax.ppermute(far, axis, far_pairs)  3.4 us
    pallas_call x1, Pallas kernels, body(): pl.pallas_call(load_kernel, out_shape=(padded_block, edge_rows, edge_rows...  2.18 us
    pallas_call x1, Pallas kernels, body(): pl.pallas_call(move_kernel, out_shape=jax.ShapeDtypeStruct(state.shape, j...  1.82 us
    ppermute x4, waiting for transfers between devices, shift(): lax.ppermute(array, axis, [(i, (i + step) % devices) for i in range(devic...  1.68 us
    pallas_call x1, Pallas kernels, body(): pl.pallas_call(answers_kernel, out_shape=(answer, answer, padded_block),...  1.23 us
    pallas_call x1, Pallas kernels, body(): pl.pallas_call(own_boxes_kernel, out_shape=box_tables, in_specs=[in_smem(...  0.76 us
    pallas_call x1, Pallas kernels, body(): pl.pallas_call(halo_boxes_kernel, out_shape=(box_tables, padded_block), i...  0.5 us
  transfers between devices with their start and end apart: 6, of which 3 were waited for; matrix products, arithmetic and copies ran while one was open for 0% of the time, Pallas kernels for 6%

profile of v1, /device:TPU:0, one launch (start us, length us, event | category | flops | bytes accessed | tf_op | source)
XLA Modules:
  0.0 20.3 jit_solution(9299980320071248146)
XLA Ops:
  0.0 2.2 %load.1 = (f32[3,16,4,48,128]{4,3,2,1,0:T(8,128)S(1)}, f32[3,16,2,512]{3,2,1,0:T(2,128)S(1)}, f32[3,16,2,512]{3,2,1,0:T(2,128)S(1)}, s32[3,32]{1,0:T(4,128)S(4)}) custom-call(f32[3,16,32,512]{3,2,1,0:T(8,128)} %field.1, s32[3,32]{1,0:T(4,128)} %bitcast.4), custom_call_target="tpu_custom_call" | custom-call | tf_op jit(solution)/shard_map/load/pallas_call | solution.py:359
  2.2 3.4 %collective-permute-start = (f32[3,16,2,512]{3,2,1,0:T(2,128)S(1)}, f32[3,16,2,512]{3,2,1,0:T(2,128)S(1)}, u32[]{:S(2)}, u32[]{:S(2)}) collective-permute-start(f32[3,16,2,512]{3,2,1,0:T(2,128)S(1)} %get-tuple-element.14), channel_id=1, source_target_pairs={{0,7},{1,2},{2,1},{3,4},{4,3},{5,6},{6,5},{7,0},{8,15},{9,10},{10,... | collective-permute-start | bytes 589832 | tf_op jit(solution)/shard_map/ppermute | solution.py:337
  5.6 0.0 collective-permute-start.1
  5.6 1.6 %collective-permute-start.3 = (s32[3,32]{1,0:T(4,128)}, s32[3,32]{1,0:T(4,128)S(1)}, u32[]{:S(2)}, u32[]{:S(2)}) collective-permute-start(s32[3,32]{1,0:T(4,128)} %bitcast.5), channel_id=1, source_target_pairs={{0,8},{8,16},{16,24},{24,0},{1,9},{9,17},{17,25},{25,1},{2,10},{10... | collective-permute-start | bytes 1160 | tf_op jit(solution)/shard_map/ppermute | solution.py:343
  7.2 2.2 %collective-permute-start.2 = (s32[3,32]{1,0:T(4,128)}, s32[3,32]{1,0:T(4,128)S(1)}, u32[]{:S(2)}, u32[]{:S(2)}) collective-permute-start(s32[3,32]{1,0:T(4,128)} %bitcast.6), channel_id=1, source_target_pairs={{0,24},{8,0},{16,8},{24,16},{1,25},{9,1},{17,9},{25,17},{2,26},{10... | collective-permute-start | bytes 1160 | tf_op jit(solution)/shard_map/ppermute | solution.py:343
  10.1 0.8 %own_boxes.1.before.partial = f32[4,16,128]{2,1,0:T(8,128)S(1)} custom-call(s32[3,32]{1,0:T(4,128)S(4)} %get-tuple-element.13.table, s32[1]{0:T(128)S(6)} %copy.10.live, f32[3,16,4,48,128]{4,3,2,1,0:T(8,128)S(1)} %get-tuple-element.16.padded.padded_in), custom_call_target="tpu_custom_call" | custom-call | flops 1000000 | bytes 8000000 | tf_op jit(solution)/shard_map/own_boxes/pallas_call | solution.py:376
  10.8 0.0 copy-start
  10.8 0.0 copy-start.1
  10.8 0.3 %collective-permute-done.3.lower_table = s32[3,32]{1,0:T(4,128)S(1)} collective-permute-done((s32[3,32]{1,0:T(4,128)}, s32[3,32]{1,0:T(4,128)S(1)}, u32[]{:S(2)}, u32[]{:S(2)}) %collective-permute-start.3) | collective-permute-done | bytes 416 | tf_op jit(solution)/shard_map/ppermute | solution.py:343
  11.2 0.0 collective-permute-done.2.upper_table
  11.2 0.0 collective-permute-done.far
  11.2 0.0 collective-permute-done.1.near
  11.2 1.2 %answers.1 = (f32[4,8,128]{2,1,0:T(8,128)S(1)}, f32[4,8,128]{2,1,0:T(8,128)S(1)}, f32[3,16,4,48,128]{4,3,2,1,0:T(8,128)S(1)}) custom-call(s32[3,32]{1,0:T(4,128)S(1)} %collective-permute-done.2.upper_table, s32[3,32]{1,0:T(4,128)S(1)} %collective-permute-done.3.lower_table, ...), custom_call_target="tpu_custom_call", output_to_operand_aliasing={{2}: (2, {})} | custom-call | tf_op jit(solution)/shard_map/answers/pallas_call | solution.py:387
  12.4 2.3 %collective-permute-start.4 = (f32[4,8,128]{2,1,0:T(8,128)S(1)}, f32[4,8,128]{2,1,0:T(8,128)S(1)}, u32[]{:S(2)}, u32[]{:S(2)}) collective-permute-start(f32[4,8,128]{2,1,0:T(8,128)S(1)} %get-tuple-element.19), channel_id=1, source_target_pairs={{0,8},{8,16},{16,24},{24,0},{1,9},{9,17},{17,25},{25,1},{2,10},{10... | collective-permute-start | bytes 49160 | tf_op jit(solution)/shard_map/ppermute | solution.py:343
  14.7 2.0 %collective-permute-start.5 = (f32[4,8,128]{2,1,0:T(8,128)S(1)}, f32[4,8,128]{2,1,0:T(8,128)S(1)}, u32[]{:S(2)}, u32[]{:S(2)}) collective-permute-start(f32[4,8,128]{2,1,0:T(8,128)S(1)} %get-tuple-element.20), channel_id=1, source_target_pairs={{0,24},{8,0},{16,8},{24,16},{1,25},{9,1},{17,9},{25,17},{2,26},{10... | collective-permute-start | bytes 49160 | tf_op jit(solution)/shard_map/ppermute | solution.py:343
  16.7 0.5 %halo_boxes.1 = (f32[4,16,128]{2,1,0:T(8,128)S(1)}, f32[3,16,4,48,128]{4,3,2,1,0:T(8,128)S(1)}) custom-call(s32[3,32]{1,0:T(4,128)S(4)} %get-tuple-element.13.table, s32[1]{0:T(128)S(6)} %copy.10.live, f32[3,16,2,512]{3,2,1,0:T(2,128)S(1)} %collective-permute-done.far, ...), custom_call_target="tpu_custom_call", output_to_operand_aliasing={{1}: (5, {})} | custom-call | flops 1000000 | bytes 4000000 | tf_op jit(solution)/shard_map/halo_boxes/pallas_call | solution.py:402
  17.2 1.2 %collective-permute-done.4.from_lower = f32[4,8,128]{2,1,0:T(8,128)S(1)} collective-permute-done((f32[4,8,128]{2,1,0:T(8,128)S(1)}, f32[4,8,128]{2,1,0:T(8,128)S(1)}, u32[]{:S(2)}, u32[]{:S(2)}) %collective-permute-start.4) | collective-permute-done | bytes 16416 | tf_op jit(solution)/shard_map/ppermute | solution.py:343
  18.3 0.2 collective-permute-done.5.from_upper
  18.5 0.0 copy-done
  18.5 0.0 copy-done.1
  18.5 1.8 %move.1 = f32[6,32,256]{2,1,0:T(8,128)} custom-call(s32[1]{0:T(128)S(6)} %copy.10.live, f32[4,16,128]{2,1,0:T(8,128)S(1)} %get-tuple-element.18.box_table, f32[4,8,128]{2,1,0:T(8,128)S(1)} %collective-permute-done.4.from_lower, f32[4,8,128]{2,1,0:T(8,128)S(1)} %collective-permute-done.5.from_upper, f32[6,32,256]{2,1,0:T(8,128)S(1)} %bitcast.3, ...), custom_call_target="tpu_custom_call" | custom-call | tf_op jit(solution)/shard_map/move/pallas_call | solution.py:414
Async XLA Ops:
  2.2 9.0 %collective-permute-start = (f32[3,16,2,512]{3,2,1,0:T(2,128)S(1)}, f32[3,16,2,512]{3,2,1,0:T(2,128)S(1)}, u32[]{:S(2)}, u32[]{:S(2)}) collective-permute-start(f32[3,16,2,512]{3,2,1,0:T(2,128)S(1)} %get-tuple-element.14), channel_id=1, source_target_pairs={{0,7},{1,2},{2,1},{3,4},{4,3},{5,6},{6,5},{7,0},{8,15},{9,10},{10,... | collective-permute-start | bytes 589832 | tf_op jit(solution)/shard_map/ppermute | solution.py:337
  5.6 5.6 %collective-permute-start.1 = (f32[3,16,2,512]{3,2,1,0:T(2,128)S(1)}, f32[3,16,2,512]{3,2,1,0:T(2,128)S(1)}, u32[]{:S(2)}, u32[]{:S(2)}) collective-permute-start(f32[3,16,2,512]{3,2,1,0:T(2,128)S(1)} %get-tuple-element.15), channel_id=1, source_target_pairs={{0,1},{1,0},{2,3},{3,2},{4,5},{5,4},{6,7},{7,6},{8,9},{9,8},{10,11... | collective-permute-start | bytes 589832 | tf_op jit(solution)/shard_map/ppermute | solution.py:338
  5.6 5.6 %collective-permute-start.3 = (s32[3,32]{1,0:T(4,128)}, s32[3,32]{1,0:T(4,128)S(1)}, u32[]{:S(2)}, u32[]{:S(2)}) collective-permute-start(s32[3,32]{1,0:T(4,128)} %bitcast.5), channel_id=1, source_target_pairs={{0,8},{8,16},{16,24},{24,0},{1,9},{9,17},{17,25},{25,1},{2,10},{10... | collective-permute-start | bytes 1160 | tf_op jit(solution)/shard_map/ppermute | solution.py:343
  7.2 4.0 %collective-permute-start.2 = (s32[3,32]{1,0:T(4,128)}, s32[3,32]{1,0:T(4,128)S(1)}, u32[]{:S(2)}, u32[]{:S(2)}) collective-permute-start(s32[3,32]{1,0:T(4,128)} %bitcast.6), channel_id=1, source_target_pairs={{0,24},{8,0},{16,8},{24,16},{1,25},{9,1},{17,9},{25,17},{2,26},{10... | collective-permute-start | bytes 1160 | tf_op jit(solution)/shard_map/ppermute | solution.py:343
  10.8 7.7 %copy-start = (f32[32,6,256]{2,0,1:T(8,128)S(1)}, f32[32,6,256]{2,0,1:T(8,128)}, u32[]{:S(2)}) copy-start(f32[32,6,256]{2,0,1:T(8,128)} %param.6) | copy-start | bytes 589828
  10.8 7.7 %copy-start.1 = (f32[32,256]{1,0:T(8,128)S(1)}, f32[32,256]{1,0:T(8,128)}, u32[]{:S(2)}) copy-start(f32[32,256]{1,0:T(8,128)} %stokes.1) | copy-start | bytes 98308
  12.4 5.9 %collective-permute-start.4 = (f32[4,8,128]{2,1,0:T(8,128)S(1)}, f32[4,8,128]{2,1,0:T(8,128)S(1)}, u32[]{:S(2)}, u32[]{:S(2)}) collective-permute-start(f32[4,8,128]{2,1,0:T(8,128)S(1)} %get-tuple-element.19), channel_id=1, source_target_pairs={{0,8},{8,16},{16,24},{24,0},{1,9},{9,17},{17,25},{25,1},{2,10},{10... | collective-permute-start | bytes 49160 | tf_op jit(solution)/shard_map/ppermute | solution.py:343
  14.7 3.8 %collective-permute-start.5 = (f32[4,8,128]{2,1,0:T(8,128)S(1)}, f32[4,8,128]{2,1,0:T(8,128)S(1)}, u32[]{:S(2)}, u32[]{:S(2)}) collective-permute-start(f32[4,8,128]{2,1,0:T(8,128)S(1)} %get-tuple-element.20), channel_id=1, source_target_pairs={{0,24},{8,0},{16,8},{24,16},{1,25},{9,1},{17,9},{25,17},{2,26},{10... | collective-permute-start | bytes 49160 | tf_op jit(solution)/shard_map/ppermute | solution.py:343
